TPU v7x, 256 devices: a whole 4x4x8 slice. The times are simulated.
256 devices in a mesh: occ: 16 (over z, y_lo), aux: 16 (over x, y_hi, core).
Axes of the slice: x: 4, y: 4 (y_hi: 2, y_lo: 2; y = y_hi * 2 + y_lo), z: 8, core: 2. Of those that a mesh axis runs over, the one named last changes fastest.
Arguments:
- factors: bfloat16 [16, 2048, 6144], P('occ', None, 'aux'), may hold values from -2.5 to 2.5
- eps_occ: float32 [32], replicated, may hold values from -2.5 to -0.3
- eps_vir: float32 [2048], replicated, may hold values from 0.2 to 3
- window_start: int32 [1], replicated, may hold values from 0 to 16
- assignment: int32 [16], replicated, may hold values from 0 to 15, each once
Outputs:
- gamma: float32 [16, 2048, 6144], P('occ', None, 'aux')
Inputs may be any that keep to these rules, and one draw needn't show every extreme that they name: `assignment`: each number once.
All inputs are finite; a program needn't handle non-finite values.
Results may differ from a plain program's by a relative error of at most 0.0023.
Values may be sent and summed in bfloat16 or wider, within the bound.
A program may use at most 64 MiB of HBM per device.

v0:
```python
import jax
import jax.numpy as jnp
from jax import lax
from jax.sharding import PartitionSpec as P

BLK = 512


def passed_along(shard, axis, by):
    size = lax.axis_size(axis)
    return lax.ppermute(shard, axis, [(i, (i + by) % size) for i in range(size)])


def per_device(factors, eps_occ, eps_vir, window_start, assignment):
    own = factors[0]
    groups = lax.axis_size("occ")
    here = lax.axis_index("occ")
    before = (here + groups - 1) % groups
    paired = passed_along(factors, "occ", 1)[0]

    def orbital(group):
        slot = window_start[0] + lax.dynamic_slice_in_dim(assignment, group, 1, 0)[0]
        return lax.dynamic_slice_in_dim(eps_occ, slot, 1, 0)[0]

    occ_sum = orbital(here) + orbital(before)
    width = own.shape[0]
    gamma_own = jnp.zeros(own.shape, jnp.float32)
    back_blocks = []
    for first in range(0, width, BLK):
        rows_pair = paired[first : first + BLK]
        share = lax.psum_scatter(
            lax.dot_general(
                rows_pair, own, (((1,), (1,)), ((), ())), preferred_element_type=jnp.float32
            ),
            "aux",
            scatter_dimension=0,
            tiled=True,
        )
        share_rows = share.shape[0]
        eps_rows = lax.dynamic_slice_in_dim(
            eps_vir, first + lax.axis_index("aux") * share_rows, share_rows, 0
        )
        amplitude = (share / (eps_rows[:, None] + eps_vir[None, :] - occ_sum)).astype(jnp.bfloat16)
        piece = lax.all_gather(amplitude, "aux", axis=0, tiled=True)
        own_total = gamma_own
        own_total = own_total + lax.dot_general(
            piece, rows_pair, (((0,), (0,)), ((), ())), preferred_element_type=jnp.float32
        )
        updated = jnp.dot(piece, own, preferred_element_type=jnp.float32)
        gamma_own = own_total
        back_blocks.append(updated)
    gamma_back = jnp.concatenate(back_blocks, axis=0)
    returned = passed_along(gamma_back, "occ", -1)
    return (gamma_own + returned)[None]


def solution(mesh):
    in_specs = (P("occ", None, "aux"), P(), P(), P(), P())
    out_specs = P("occ", None, "aux")
    return jax.shard_map(
        per_device, mesh=mesh, in_specs=in_specs, out_specs=out_specs, check_vma=False
    )
```

profile of v0, /device:TPU:1, one launch (start us, length us, event | category | flops | bytes accessed | tf_op | source)
XLA Modules:
  0.0 721.3 jit_solution(16708454230518948043)
XLA Ops:
  6.5 0.0 reduce-scatter.11.cloned.1.call-start
  6.5 2.1 collective-permute-start
  8.7 39.6 %collective-permute-done = bf16[1,2048,384]{2,1,0:T(8,128)(2,1)S(1)} collective-permute-done((bf16[1,2048,384]{2,1,0:T(8,128)(2,1)}, bf16[1,2048,384]{2,1,0:T(8,128)(2,1)S(1)}, u32[]{:S(2)}, u32[]{:S(2)}) %collective-permute-start) | collective-permute-done | bytes 1572896 | tf_op jit(solution)/shard_map/ppermute | solution.py:11
  48.3 4.6 fusion.8
  52.9 0.0 reduce-scatter.11.cloned.1.call-update
  53.0 0.0 reduce-scatter.5.cloned.1.call-start
  53.0 1.3 copy-done
  54.3 3.3 fusion.14
  57.7 0.0 reduce-scatter.5.cloned.1.call-update
  57.7 0.0 reduce-scatter.7.cloned.1.call-start
  57.7 3.3 fusion.12
  61.0 0.0 reduce-scatter.7.cloned.1.call-update
  61.0 0.0 reduce-scatter.9.cloned.1.call-start
  61.1 3.2 fusion.10
  64.3 0.0 reduce-scatter.9.cloned.1.call-update
  64.3 0.0 all-gather.11.cloned.1.call-start
  65.0 0.0 copy-done.9
  65.1 0.6 fusion.22
  66.9 0.6 fusion.21
  68.7 0.1 fusion.20
  68.8 71.5 %reduce-scatter.11.cloned.1.call-done = f32[32,2048]{1,0:T(8,128)} async-done(((f32[512,2048]{1,0:T(8,128)}), f32[32,2048]{1,0:T(8,128)}) %reduce-scatter.11.cloned.1.call-update) | async-done | bytes 262160 | tf_op jit(solution)/shard_map/reduce_scatter | solution.py:31
  140.3 92.0 %reduce-scatter.5.cloned.1.call-done = f32[32,2048]{1,0:T(8,128)} async-done(((f32[512,2048]{1,0:T(8,128)}), f32[32,2048]{1,0:T(8,128)}) %reduce-scatter.5.cloned.1.call-update) | async-done | bytes 262160 | tf_op jit(solution)/shard_map/reduce_scatter | solution.py:31
  232.3 91.3 %reduce-scatter.7.cloned.1.call-done = f32[32,2048]{1,0:T(8,128)} async-done(((f32[512,2048]{1,0:T(8,128)}), f32[32,2048]{1,0:T(8,128)}) %reduce-scatter.7.cloned.1.call-update) | async-done | bytes 262160 | tf_op jit(solution)/shard_map/reduce_scatter | solution.py:31
  323.6 91.9 %reduce-scatter.9.cloned.1.call-done = f32[32,2048]{1,0:T(8,128)} async-done(((f32[512,2048]{1,0:T(8,128)}), f32[32,2048]{1,0:T(8,128)}) %reduce-scatter.9.cloned.1.call-update) | async-done | bytes 262160 | tf_op jit(solution)/shard_map/reduce_scatter | solution.py:31
  415.5 2.1 divide_convert_fusion.3
  417.6 0.0 all-gather.11.cloned.1.call-update
  417.6 0.0 all-gather.9.cloned.1.call-start
  417.7 0.5 all-gather.9.cloned.1.call-update
  418.2 0.0 all-gather.7.cloned.1.call-start
  418.3 0.7 all-gather.7.cloned.1.call-update
  419.0 0.0 all-gather.5.cloned.1.call-start
  419.0 0.7 all-gather.5.cloned.1.call-update
  419.7 52.5 %all-gather.11.cloned.1.call-done = bf16[512,2048]{1,0:T(8,128)(2,1)} async-done(((bf16[32,2048]{1,0:T(8,128)(2,1)}), bf16[512,2048]{1,0:T(8,128)(2,1)}) %all-gather.11.cloned.1.call-update) | async-done | bytes 2097168 | tf_op jit(solution)/shard_map/all_gather | solution.py:44
  472.3 3.7 fusion
  476.0 51.2 %all-gather.9.cloned.1.call-done = bf16[512,2048]{1,0:T(8,128)(2,1)} async-done(((bf16[32,2048]{1,0:T(8,128)(2,1)}), bf16[512,2048]{1,0:T(8,128)(2,1)}) %all-gather.9.cloned.1.call-update) | async-done | bytes 2097168 | tf_op jit(solution)/shard_map/all_gather | solution.py:44
  527.2 3.8 fusion.2
  531.0 51.3 %all-gather.7.cloned.1.call-done = bf16[512,2048]{1,0:T(8,128)(2,1)} async-done(((bf16[32,2048]{1,0:T(8,128)(2,1)}), bf16[512,2048]{1,0:T(8,128)(2,1)}) %all-gather.7.cloned.1.call-update) | async-done | bytes 2097168 | tf_op jit(solution)/shard_map/all_gather | solution.py:44
  582.3 3.7 fusion.4
  586.0 51.4 %all-gather.5.cloned.1.call-done = bf16[512,2048]{1,0:T(8,128)(2,1)} async-done(((bf16[32,2048]{1,0:T(8,128)(2,1)}), bf16[512,2048]{1,0:T(8,128)(2,1)}) %all-gather.5.cloned.1.call-update) | async-done | bytes 2097168 | tf_op jit(solution)/shard_map/all_gather | solution.py:44
  637.4 3.0 fusion.6
  640.4 0.2 pad_maximum_fusion
  640.6 3.3 collective-permute-start.1
  643.9 1.3 fusion.16
  645.3 1.3 fusion.17
  646.6 0.3 copy-done.1
  646.9 1.3 fusion.18
  648.2 63.0 %collective-permute-done.1 = f32[2048,384]{1,0:T(8,128)S(1)} collective-permute-done((f32[2048,384]{1,0:T(8,128)S(1)}, f32[2048,384]{1,0:T(8,128)S(1)}, u32[]{:S(2)}, u32[]{:S(2)}) %collective-permute-start.1) | collective-permute-done | bytes 3145760 | tf_op jit(solution)/shard_map/ppermute | solution.py:11
  711.2 3.3 add_bitcast_fusion
  (19 shorter events, 0.0 us)
Async XLA Ops:
  6.5 133.8 %reduce-scatter.11.cloned.1.call-start = ((), (), s32[]{:S(2)}) async-start(), calls=%async_computation.10 | async-start | bytes 4456448 | tf_op jit(solution)/shard_map/reduce_scatter | solution.py:31
  6.5 41.7 %collective-permute-start = (bf16[1,2048,384]{2,1,0:T(8,128)(2,1)}, bf16[1,2048,384]{2,1,0:T(8,128)(2,1)S(1)}, u32[]{:S(2)}, u32[]{:S(2)}) collective-permute-start(bf16[1,2048,384]{2,1,0:T(8,128)(2,1)} %param.5), channel_id=1, source_target_pairs={{0,16},{16,32},{32,48},{48,64},{64,80},{80,96},{96,112},{112,128},... | collective-permute-start | bytes 4718600 | tf_op jit(solution)/shard_map/ppermute | solution.py:11
  52.9 1.4 copy-start
  53.0 179.4 %reduce-scatter.5.cloned.1.call-start = ((), (), s32[]{:S(2)}) async-start(), calls=%async_computation.4 | async-start | bytes 4456448 | tf_op jit(solution)/shard_map/reduce_scatter | solution.py:31
  57.7 265.9 %reduce-scatter.7.cloned.1.call-start = ((), (), s32[]{:S(2)}) async-start(), calls=%async_computation.6 | async-start | bytes 4456448 | tf_op jit(solution)/shard_map/reduce_scatter | solution.py:31
  61.0 354.5 %reduce-scatter.9.cloned.1.call-start = ((), (), s32[]{:S(2)}) async-start(), calls=%async_computation.8 | async-start | bytes 4456448 | tf_op jit(solution)/shard_map/reduce_scatter | solution.py:31
  64.3 0.7 copy-start.9
  64.3 2.6 copy-start.10
  64.3 4.4 copy-start.8
  64.3 407.9 %all-gather.11.cloned.1.call-start = ((), (), s32[]{:S(2)}) async-start(), calls=%async_computation.11 | async-start | bytes 2228224 | tf_op jit(solution)/shard_map/all_gather | solution.py:44
  417.6 109.6 %all-gather.9.cloned.1.call-start = ((), (), s32[]{:S(2)}) async-start(), calls=%async_computation.9 | async-start | bytes 2228224 | tf_op jit(solution)/shard_map/all_gather | solution.py:44
  418.2 164.1 %all-gather.7.cloned.1.call-start = ((), (), s32[]{:S(2)}) async-start(), calls=%async_computation.7 | async-start | bytes 2228224 | tf_op jit(solution)/shard_map/all_gather | solution.py:44
  419.0 218.4 %all-gather.5.cloned.1.call-start = ((), (), s32[]{:S(2)}) async-start(), calls=%async_computation.5 | async-start | bytes 2228224 | tf_op jit(solution)/shard_map/all_gather | solution.py:44
  637.4 3.0 copy-start.5
  637.4 3.0 copy-start.6
  637.4 3.0 copy-start.7
  640.4 3.5 copy-start.3
  640.6 4.6 copy-start.2
  640.6 70.6 %collective-permute-start.1 = (f32[2048,384]{1,0:T(8,128)S(1)}, f32[2048,384]{1,0:T(8,128)S(1)}, u32[]{:S(2)}, u32[]{:S(2)}) collective-permute-start(f32[2048,384]{1,0:T(8,128)S(1)} %pad_maximum_fusion), channel_id=1, source_target_pairs={{0,240},{16,0},{32,16},{48,32},{64,48},{80,64},{96,80},{112,96},{1... | collective-permute-start | bytes 9437192 | tf_op jit(solution)/shard_map/ppermute | solution.py:11
  645.3 1.6 copy-start.1
  646.9 64.3 %copy-start.4 = (bf16[512,2048]{1,0:T(8,128)(2,1)S(1)}, bf16[512,2048]{1,0:T(8,128)(2,1)}, u32[]{:S(2)}) copy-start(bf16[512,2048]{1,0:T(8,128)(2,1)} %all-gather.11.cloned.1.call-done) | copy-start | bytes 6291460
Sparse Core Ops, SparseCore 0:
  53.1 87.1 reduce-scatter.10
  145.3 87.0 reduce-scatter.4
  236.7 86.9 reduce-scatter.6
  328.4 87.0 reduce-scatter.8
  418.0 54.1 all-gather.10
  474.8 52.3 all-gather.8
  529.9 52.3 all-gather.6
  585.0 52.3 all-gather.4
where the time goes:
time: 722 us; the launch traced here: 721 us
  waiting for transfers between devices  658 us (91%)
  matrix products  35.9 us (5%)
  between operations  16.7 us (2%)
    reduce_scatter x4, waiting for transfers between devices, per_device(): lax.psum_scatter(lax.dot_general(rows_pair, own, (((1,), (1,)), ((), ()))...  347 us
    all_gather x4, waiting for transfers between devices, per_device(): piece = lax.all_gather(amplitude, 'aux', axis=0, tiled=True)  206 us
    ppermute x2, waiting for transfers between devices, passed_along(): lax.ppermute(shard, axis, [(i, (i + by) % size) for i in range(size)])  103 us
    dot_general x4, matrix products, per_device(): lax.dot_general(rows_pair, own, (((1,), (1,)), ((), ())), preferred_eleme...  14.5 us
  transfers between devices with their start and end apart: 10, of which 10 were waited for; matrix products, arithmetic and copies ran while one was open for 4% of the time, Pallas kernels for 0%

commit v1 on v0

v1 whole, which is shorter than its diff:
```python
import functools

import jax
import jax.numpy as jnp
from jax import lax
from jax.experimental import pallas as pl
from jax.experimental.pallas import tpu as pltpu
from jax.sharding import PartitionSpec as P

MESH = pl.DeviceIdType.MESH
NX, NY, NC = 4, 2, 2
BLOCKS = NX * NY
Y_LO, Y_ALL = 2, 4
ROWS = 64
PART = 128
GROUP = 256
AHEAD = 2


def dot(a, b, dims):
    return lax.dot_general(a, b, (dims, ((), ())), preferred_element_type=jnp.float32)


def kernel(
    n_occ, rows, eps_occ, start, assignment, own, eps_vir, out,
    left, right, tile, far_out, far, near, tail_via, tail, amp_via, amp, acc, back, back_in, acc_in, eps_rows, right_last, amp_last,
    local_sem, left_sem, right_sem, far_sem, near_sem, tail_sem, tail_via_sem,
    amp_y_sem, amp_y_via_sem, amp_x_sem, amp_f_sem, back_sem, acc_sem, right_last_sem, amp_last_sem,
):
    v, k = own.shape
    half_v = v // NC
    width = v // BLOCKS
    n = half_v // rows
    half = rows // 2
    per_part, per_group = PART // rows, GROUP // rows
    parts, first_last = half_v // PART, half_v - GROUP

    o = lax.axis_index("occ")
    u = lax.axis_index("aux")
    x, y, core = u // (NY * NC), (u // NC) % NY, u % NC
    o_next, o_prev = lax.rem(o + 1, n_occ), lax.rem(o + n_occ - 1, n_occ)
    x_next, x_prev, x_far = lax.rem(x + 1, NX), lax.rem(x + NX - 1, NX), lax.rem(x + 2, NX)

    def at(o_, x_, y_, c_):
        return (o_, (x_ * NY + y_) * NC + c_)

    sibling = at(o, x, y, 1 - core)

    def across(step):
        place = lax.rem(y * Y_LO + lax.rem(o, Y_LO) + step + Y_ALL, Y_ALL)
        return at((o // Y_LO) * Y_LO + lax.rem(place, Y_LO), x, place // Y_LO, core), place // Y_LO

    hop, _ = across(1 - 2 * core)
    hop_back, from_y = across(2 * core - 1)
    x_dev = (at(o, x_next, y, core), at(o, x_prev, y, core))
    next_dev = (at(o_next, x, y, 0), at(o_next, x, y, 1))
    prev_dev = (at(o_prev, x, y, 0), at(o_prev, x, y, 1))
    mine, theirs = x * NY + y, x * NY + 1 - y

    def remote(src, dst, sem, device, there=None):
        return pltpu.make_async_remote_copy(
            src_ref=src, dst_ref=dst, send_sem=sem.at[0], recv_sem=(sem if there is None else there).at[1],
            device_id=device, device_id_type=MESH,
        )

    def rds(c, size=rows, offset=0):
        return pl.ds(pl.multiple_of(c * rows + offset, 16), size)

    cols = lambda c_: pl.ds(pl.multiple_of(c_ * k, 128), k)
    pair_of = lambda x_: pl.ds(x_ * NY, NY)

    def left_copy():
        return remote(own, left.at[:, cols(core)], left_sem, sibling)

    def prds(p):
        return pl.ds(pl.multiple_of(p * PART, 16), PART)

    def right_copy(p, d):
        src = own.at[pl.ds(pl.multiple_of(d * half_v + p * PART, 16), PART), :]
        return remote(
            src, right.at[prds(p), cols(core)], right_sem.at[p, d], next_dev[d], right_sem.at[p, core]
        )

    def right_arrival(p, s):
        src = own.at[pl.ds(0, PART), :]
        return remote(src, right.at[prds(p), cols(s)], right_sem.at[p, s], next_dev[s])

    def right_last_copy(p):
        r = pl.ds(pl.multiple_of(p * PART - first_last, 16), PART)
        i = p - first_last // PART
        return remote(right.at[prds(p), cols(1 - core)], right_last.at[r, :], right_last_sem.at[i], sibling)

    def far_copy(c, d):
        r = rds(c, half, d * half)
        return remote(far_out.at[:, r, :], far.at[:, r, :], far_sem.at[c, d], x_dev[d])

    def near_copy(c, d):
        src = tile.at[pair_of((x_next, x_prev)[d]), rds(c), :]
        return remote(src, near.at[d, :, rds(c), :], near_sem.at[c, d], x_dev[d])

    def tail_copy(c):
        return remote(tile.at[theirs, rds(c), :], tail_via.at[rds(c), :], tail_via_sem.at[c], hop)

    def tail_pass(c):
        return remote(tail_via.at[rds(c), :], tail.at[rds(c), :], tail_sem.at[c], hop)

    def amp_y_copy(c):
        return remote(amp.at[mine, rds(c), :], amp_via.at[rds(c), :], amp_y_via_sem.at[c], hop)

    def amp_y_pass(c, block):
        return remote(amp_via.at[rds(c), :], amp.at[block, rds(c), :], amp_y_sem.at[c], hop)

    def amp_x_copy(c, d, x_=x):
        block = amp.at[pair_of(x_), rds(c), :]
        return remote(block, block, amp_x_sem.at[c, d], x_dev[d])

    def amp_f_copy(c, d, x_):
        block = amp.at[pair_of(x_), rds(c, half, d * half), :]
        return remote(block, block, amp_f_sem.at[c, d], x_dev[d])

    def amp_last_copy(c):
        r = pl.ds(pl.multiple_of(c * rows - first_last, 16), rows)
        return remote(amp.at[:, rds(c), :], amp_last.at[:, r, :], amp_last_sem.at[c - (n - per_group)], sibling)

    def back_copy(p, d):
        dst = back_in.at[pl.ds(pl.multiple_of(core * half_v + p * PART, 16), PART), :]
        return remote(back.at[prds(p), cols(d)], dst, back_sem.at[p, d], prev_dev[d], back_sem.at[p, core])

    def back_arrival(p, s):
        dst = back_in.at[pl.ds(pl.multiple_of(s * half_v + p * PART, 16), PART), :]
        return remote(back.at[prds(p), cols(s)], dst, back_sem.at[p, s], prev_dev[s])

    def acc_copy(b):
        return remote(acc.at[b, :, cols(1 - core)], acc_in.at[b], acc_sem.at[b], sibling)

    barrier = pltpu.get_barrier_semaphore()
    others = (sibling, hop, hop_back) + x_dev + next_dev + prev_dev
    for device in others:
        pl.semaphore_signal(barrier, inc=1, device_id=device, device_id_type=MESH)
    local = pltpu.make_async_copy(own, left.at[:, cols(core)], local_sem)
    local.start()

    for i in range(half_v // min(128, half_v)):
        m = min(128, half_v)
        line = eps_vir[:, pl.ds(pl.multiple_of(core * half_v + i * m, m), m)]
        eps_rows[pl.ds(i * m, m), :] = jnp.broadcast_to(line, (m, m)).T
    for b in range(BLOCKS):
        acc[b] = jnp.zeros((width, NC * k), jnp.float32)
    slot = start[0]
    occ_sum = eps_occ[slot + assignment[o]] + eps_occ[slot + assignment[o_prev]]
    eps_cols = eps_vir[:, pl.ds(pl.multiple_of(mine * width, width), width)] - occ_sum

    pl.semaphore_wait(barrier, len(others))

    def send_right(p):
        for d in range(NC):
            right_copy(p, d).start()

    left_copy().start()
    for p in range(min(AHEAD, parts)):
        send_right(p)
    local.wait()
    left_copy().wait_recv()

    def tile_block(p, x_):
        block = left[pl.ds(pl.multiple_of(x_ * NY * width, NY * width), NY * width), :]
        return dot(right[prds(p), :], block, ((1,), (1,)))

    def stage_tile(c):
        p = c // per_part

        @pl.when(lax.rem(c, per_part) == 0)
        def _():
            @pl.when(p + AHEAD < parts)
            def _():
                send_right(p + AHEAD)

            for s in range(NC):
                right_arrival(p, s).wait_recv()

            @pl.when(p >= first_last // PART)
            def _():
                right_last_copy(p).start()

            values = tile_block(p, x_far).astype(jnp.bfloat16)
            for j in range(NY):
                far_out[j, prds(p), :] = values[:, j * width : (j + 1) * width]

        for d in range(2):
            far_copy(c, d).start()

        @pl.when(lax.rem(c, per_part) == 0)
        def _():
            for x_ in (x_next, x_prev, x):
                values = tile_block(p, x_)
                for j in range(NY):
                    tile[x_ * NY + j, prds(p), :] = values[:, j * width : (j + 1) * width]

    def stage_near(c):
        for d in range(2):
            far_copy(c, d).wait_recv()
            x_ = (x_next, x_prev)[d]
            r = rds(c, half, d * half)
            for j in range(NY):
                tile[x_ * NY + j, r, :] += far[j, r, :].astype(jnp.float32)
        for d in range(2):
            near_copy(c, d).start()

    def stage_sum(c):
        for d in range(2):
            near_copy(c, d).wait_recv()
        r = rds(c)
        tile[theirs, r, :] += near[0, 1 - y, r, :] + near[1, 1 - y, r, :]
        tail_copy(c).start()
        tile[mine, r, :] += near[0, y, r, :] + near[1, y, r, :]

    def stage_tail(c):
        tail_copy(c).wait_recv()
        tail_pass(c).start()

    def stage_amp(c):
        tail_pass(c).wait_recv()
        r = rds(c)
        total = tile[mine, r, :] + tail[r, :]
        denominator = eps_rows[r, 0:1] + eps_cols
        amp[mine, r, :] = (total / denominator).astype(jnp.bfloat16)
        amp_y_copy(c).start()

    def stage_amp_pass(c):
        amp_y_copy(c).wait_recv()
        amp_y_pass(c, x * NY + from_y).start()

    def stage_spread(c):
        amp_y_pass(c, theirs).wait_recv()
        for d in range(2):
            amp_x_copy(c, d).start()

    def stage_forward(c):
        for d in range(2):
            amp_x_copy(c, d, (x_prev, x_next)[d]).wait_recv()
            amp_f_copy(c, d, (x_prev, x_next)[d]).start()

    def own_block(first, b):
        r = pl.ds(pl.multiple_of(first * rows, 16), GROUP)
        acc[b] += dot(amp[b, r, :], right[r, :], ((0,), (0,)))

    def stage_gamma(c):
        for d in range(2):
            amp_f_copy(c, d, x_far).wait_recv()

        @pl.when(c >= n - per_group)
        def _():
            amp_last_copy(c).start()

        @pl.when(lax.rem(c + 1, per_part) == 0)
        def _():
            p = c // per_part
            r = prds(p)
            total = dot(amp[0, r, :], left[pl.ds(0, width), :], ((1,), (0,)))
            for b in range(1, BLOCKS):
                total += dot(amp[b, r, :], left[pl.ds(b * width, width), :], ((1,), (0,)))
            back[r, :] = total.astype(jnp.bfloat16)
            for d in range(NC):
                back_copy(p, d).start()

        @pl.when((lax.rem(c + 1, per_group) == 0) & (c + 1 < n))
        def _():
            for b in range(BLOCKS):
                own_block(c + 1 - per_group, b)

            @pl.when(c + 1 == n - per_group)
            def _():
                for b in range(BLOCKS):
                    acc_copy(b).start()

    stages = (
        stage_tile, stage_gamma, stage_forward, stage_spread, stage_amp_pass, stage_amp, stage_tail, stage_sum, stage_near,
    )
    offsets = (0, 16, 14, 12, 10, 8, 6, 4, 2)

    def tick(t, carry):
        for stage, offset in zip(stages, offsets):
            c = t - offset

            @pl.when((c >= 0) & (c < n))
            def _():
                stage(c)

        return carry

    lax.fori_loop(0, n + max(offsets), tick, 0)

    for p in range(first_last // PART, parts):
        right_last_copy(p).wait_recv()
    for c in range(n - per_group, n):
        amp_last_copy(c).wait_recv()
    for b in range(BLOCKS):
        acc_copy(b).wait_recv()

    last = pl.ds(first_last, GROUP)
    for b in range(BLOCKS):
        total = acc[b, :, cols(core)] + acc_in[b]
        total += dot(amp[b, last, :], right[last, cols(core)], ((0,), (0,)))
        total += dot(amp_last[b], right_last[...], ((0,), (0,)))
        out[pl.ds(b * width, width), :] = total

    def arrived(p, carry):
        for s in range(NC):
            back_arrival(p, s).wait_recv()
        return carry

    lax.fori_loop(0, parts, arrived, 0)
    for b in range(BLOCKS):
        r = pl.ds(b * width, width)
        out[r, :] += back_in[r, :].astype(jnp.float32)

    left_copy().wait_send()
    for b in range(BLOCKS):
        acc_copy(b).wait_send()
    for p in range(first_last // PART, parts):
        right_last_copy(p).wait_send()
    for c in range(n - per_group, n):
        amp_last_copy(c).wait_send()

    def part_sent(p, carry):
        for d in range(NC):
            right_copy(p, d).wait_send()
            back_copy(p, d).wait_send()
        return carry

    lax.fori_loop(0, parts, part_sent, 0)

    def sent(c, carry):
        for d in range(2):
            far_copy(c, d).wait_send()
            near_copy(c, d).wait_send()
            amp_x_copy(c, d).wait_send()
            amp_f_copy(c, d, (x_prev, x_next)[d]).wait_send()
        tail_copy(c).wait_send()
        tail_pass(c).wait_send()
        amp_y_copy(c).wait_send()
        amp_y_pass(c, x * NY + from_y).wait_send()
        return carry

    lax.fori_loop(0, n, sent, 0)


def per_device(n_occ, rows, factors, eps_occ, eps_vir, window_start, assignment):
    own = factors[0]
    v, k = own.shape
    half_v, width = v // NC, v // BLOCKS
    n = half_v // rows
    f32, bf16 = jnp.float32, jnp.bfloat16
    dma = pltpu.SemaphoreType.DMA
    smem = pl.BlockSpec(memory_space=pltpu.SMEM)
    out = pl.pallas_call(
        functools.partial(kernel, n_occ, rows),
        out_shape=jax.ShapeDtypeStruct((v, k), f32),
        in_specs=[smem, smem, smem, pl.BlockSpec(memory_space=pl.ANY), pl.BlockSpec(memory_space=pltpu.VMEM)],
        out_specs=pl.BlockSpec(memory_space=pltpu.VMEM),
        scratch_shapes=[
            pltpu.VMEM((v, NC * k), bf16),
            pltpu.VMEM((half_v, NC * k), bf16),
            pltpu.VMEM((BLOCKS, half_v, width), f32),
            pltpu.VMEM((NY, half_v, width), bf16),
            pltpu.VMEM((NY, half_v, width), bf16),
            pltpu.VMEM((2, NY, half_v, width), f32),
            pltpu.VMEM((half_v, width), f32),
            pltpu.VMEM((half_v, width), f32),
            pltpu.VMEM((half_v, width), bf16),
            pltpu.VMEM((BLOCKS, half_v, width), bf16),
            pltpu.VMEM((BLOCKS, width, NC * k), f32),
            pltpu.VMEM((half_v, NC * k), bf16),
            pltpu.VMEM((v, k), bf16),
            pltpu.VMEM((BLOCKS, width, k), f32),
            pltpu.VMEM((half_v, min(128, half_v)), f32),
            pltpu.VMEM((GROUP, k), bf16),
            pltpu.VMEM((BLOCKS, GROUP, width), bf16),
            dma(()),
            dma((2,)),
            dma((half_v // PART, 2, 2)),
            dma((n, 2, 2)),
            dma((n, 2, 2)),
            dma((n, 2)),
            dma((n, 2)),
            dma((n, 2)),
            dma((n, 2)),
            dma((n, 2, 2)),
            dma((n, 2, 2)),
            dma((half_v // PART, 2, 2)),
            dma((BLOCKS, 2)),
            dma((GROUP // PART, 2)),
            dma((GROUP // rows, 2)),
        ],
        compiler_params=pltpu.CompilerParams(
            collective_id=0, has_side_effects=True, vmem_limit_bytes=60 * 2**20
        ),
        cost_estimate=pl.CostEstimate(
            flops=3 * 2 * v * v * k, bytes_accessed=6 * v * k, transcendentals=0
        ),
    )(eps_occ, window_start, assignment, own, eps_vir[None, :])
    return out[None]


def solution(mesh):
    in_specs = (P("occ", None, "aux"), P(), P(), P(), P())
    out_specs = P("occ", None, "aux")
    return jax.shard_map(
        functools.partial(per_device, mesh.shape["occ"], ROWS),
        mesh=mesh, in_specs=in_specs, out_specs=out_specs, check_vma=False,
    )
```

time: 722 us -> 144 us (0.20)
  waiting for transfers between devices: 658 us -> 0 us
  Pallas kernels: 0 us -> 139 us
  matrix products: 35.9 us -> 0 us
  between operations: 16.7 us -> 0.66 us
    reduce_scatter x4 -> x0, waiting for transfers between devices: 347 us -> none  [per_device(): lax.psum_scatter(lax.dot_general(rows_pair, own, (((1,), (1,)), ((), ()))...]
    all_gather x4 -> x0, waiting for transfers between devices: 206 us -> none  [per_device(): piece = lax.all_gather(amplitude, 'aux', axis=0, tiled=True)]
    pallas_call x0 -> x1, Pallas kernels: none -> 139 us  [per_device(): pl.pallas_call(functools.partial(kernel, n_occ, rows), out_shape=jax.Shap...]
    ppermute x2 -> x0, waiting for transfers between devices: 103 us -> none  [passed_along(): lax.ppermute(shard, axis, [(i, (i + by) % size) for i in range(size)])]
    dot_general x12 -> x0, matrix products: 35.9 us -> none  [the longest x4 14.5 us: per_device(): lax.dot_general(rows_pair, own, (((1,), (1,)), ((), ())), preferred_eleme...]
  transfers between devices with their start and end apart: 10 -> 0, of which waited for: 10 -> 0; matrix products, arithmetic and copies ran while one was open for 4% -> 0% of each run, Pallas kernels for 0% -> 0%
where the time goes in v1:
time: 144 us
  Pallas kernels  139 us (97%)
  local copies, waits for them, and re-layouts  3.76 us (3%)
    pallas_call x1, Pallas kernels, per_device(): pl.pallas_call(functools.partial(kernel, n_occ, rows), out_shape=jax.Shap...  139 us
    unnamed x1, local copies, waits for them, and re-layouts  3.76 us

profile of v1, /device:TPU:1, one launch (start us, length us, event | category | flops | bytes accessed | tf_op | source)
XLA Modules:
  0.0 143.9 jit_solution(9535434137261155324)
XLA Ops:
  0.7 139.5 %shard_map.55 = f32[2048,384]{1,0:T(8,128)} custom-call(f32[32]{0:T(128)} %eps_occ.1, s32[1]{0:T(128)S(6)} %copy.7.start, s32[16]{0:T(128)} %assignment.1, bf16[2048,384]{1,0:T(8,128)(2,1)} %bitcast.4, f32[1,2048]{1,0:T(1,128)} %bitcast.5), custom_call_target="tpu_custom_call" | custom-call | flops 9663676416 | bytes 4718592 | tf_op jit(solution)/shard_map/pallas_call | solution.py:356
  140.1 3.8 %copy.8 = f32[1,2048,384]{2,1,0:T(8,128)} copy(f32[1,2048,384]{2,1,0:T(8,128)} %bitcast.3) | data formatting | bytes 6291456

commit v2 on v1

--- a/solution.py
+++ b/solution.py
@@ -10,22 +10,30 @@
 MESH = pl.DeviceIdType.MESH
 NX, NY, NC = 4, 2, 2
 BLOCKS = NX * NY
-Y_LO, Y_ALL = 2, 4
 ROWS = 64
-PART = 128
+PART = 64
 GROUP = 256
-AHEAD = 2
+AHEAD = 4
 
 
 def dot(a, b, dims):
     return lax.dot_general(a, b, (dims, ((), ())), preferred_element_type=jnp.float32)
 
 
+def fixed(values):
+    top = functools.reduce(jnp.maximum, [jnp.abs(v) for v in values])
+    top = jnp.max(jnp.max(top, axis=0, keepdims=True), axis=1, keepdims=True)
+    top = jnp.maximum(top, 1e-30)
+    return [jnp.round(v * (32767.0 / top)).astype(jnp.int16) for v in values], top * (1 / 32767.0)
+
+
 def kernel(
     n_occ, rows, eps_occ, start, assignment, own, eps_vir, out,
-    left, right, tile, far_out, far, near, tail_via, tail, amp_via, amp, acc, back, back_in, acc_in, eps_rows, right_last, amp_last,
-    local_sem, left_sem, right_sem, far_sem, near_sem, tail_sem, tail_via_sem,
-    amp_y_sem, amp_y_via_sem, amp_x_sem, amp_f_sem, back_sem, acc_sem, right_last_sem, amp_last_sem,
+    left, right, tile, far_out, far, near_out, near, near_unit_out, near_unit,
+    tail_out, tail, tail_unit_out, tail_unit, amp, acc, back, back_in, acc_in, eps_rows, right_last, amp_last,
+    local_sem, left_sem, right_sem, far_sem, near_sem, near_unit_sem,
+    tail_sem, tail_unit_sem,
+    amp_y_sem, amp_x_sem, amp_f_sem, back_sem, acc_sem, right_last_sem, amp_last_sem,
 ):
     v, k = own.shape
     half_v = v // NC
@@ -45,13 +53,7 @@
         return (o_, (x_ * NY + y_) * NC + c_)
 
     sibling = at(o, x, y, 1 - core)
-
-    def across(step):
-        place = lax.rem(y * Y_LO + lax.rem(o, Y_LO) + step + Y_ALL, Y_ALL)
-        return at((o // Y_LO) * Y_LO + lax.rem(place, Y_LO), x, place // Y_LO, core), place // Y_LO
-
-    hop, _ = across(1 - 2 * core)
-    hop_back, from_y = across(2 * core - 1)
+    partner = at(o, x, 1 - y, core)
     x_dev = (at(o, x_next, y, core), at(o, x_prev, y, core))
     next_dev = (at(o_next, x, y, 0), at(o_next, x, y, 1))
     prev_dev = (at(o_prev, x, y, 0), at(o_prev, x, y, 1))
@@ -95,20 +97,20 @@
         return remote(far_out.at[:, r, :], far.at[:, r, :], far_sem.at[c, d], x_dev[d])
 
     def near_copy(c, d):
-        src = tile.at[pair_of((x_next, x_prev)[d]), rds(c), :]
-        return remote(src, near.at[d, :, rds(c), :], near_sem.at[c, d], x_dev[d])
+        return remote(near_out.at[d, :, rds(c), :], near.at[d, :, rds(c), :], near_sem.at[c, d], x_dev[d])
+
+    def near_unit_copy(c, d):
+        return remote(near_unit_out.at[c, d], near_unit.at[c, d], near_unit_sem.at[c, d], x_dev[d])
 
     def tail_copy(c):
-        return remote(tile.at[theirs, rds(c), :], tail_via.at[rds(c), :], tail_via_sem.at[c], hop)
-
-    def tail_pass(c):
-        return remote(tail_via.at[rds(c), :], tail.at[rds(c), :], tail_sem.at[c], hop)
-
-    def amp_y_copy(c):
-        return remote(amp.at[mine, rds(c), :], amp_via.at[rds(c), :], amp_y_via_sem.at[c], hop)
-
-    def amp_y_pass(c, block):
-        return remote(amp_via.at[rds(c), :], amp.at[block, rds(c), :], amp_y_sem.at[c], hop)
+        return remote(tail_out.at[rds(c), :], tail.at[rds(c), :], tail_sem.at[c], partner)
+
+    def tail_unit_copy(c):
+        return remote(tail_unit_out.at[c], tail_unit.at[c], tail_unit_sem.at[c], partner)
+
+    def amp_y_copy(c, block=mine):
+        block = amp.at[block, rds(c), :]
+        return remote(block, block, amp_y_sem.at[c], partner)
 
     def amp_x_copy(c, d, x_=x):
         block = amp.at[pair_of(x_), rds(c), :]
@@ -134,7 +136,7 @@
         return remote(acc.at[b, :, cols(1 - core)], acc_in.at[b], acc_sem.at[b], sibling)
 
     barrier = pltpu.get_barrier_semaphore()
-    others = (sibling, hop, hop_back) + x_dev + next_dev + prev_dev
+    others = (sibling, partner) + x_dev + next_dev + prev_dev
     for device in others:
         pl.semaphore_signal(barrier, inc=1, device_id=device, device_id_type=MESH)
     local = pltpu.make_async_copy(own, left.at[:, cols(core)], local_sem)
@@ -203,35 +205,42 @@
             r = rds(c, half, d * half)
             for j in range(NY):
                 tile[x_ * NY + j, r, :] += far[j, r, :].astype(jnp.float32)
-        for d in range(2):
+            codes, unit = fixed([tile[x_ * NY + j, rds(c), :] for j in range(NY)])
+            for j in range(NY):
+                near_out[d, j, rds(c), :] = codes[j]
+            near_unit_out[c, d] = jnp.broadcast_to(unit, near_unit_out.shape[2:])
+            near_unit_copy(c, d).start()
             near_copy(c, d).start()
 
+    def near_sum(c, y_):
+        r = rds(c)
+        total = tile[x * NY + y_, r, :]
+        for d in range(2):
+            total += near[d, y_, r, :].astype(jnp.float32) * near_unit[c, d][0:1, 0:1]
+        return total
+
     def stage_sum(c):
         for d in range(2):
+            near_unit_copy(c, d).wait_recv()
             near_copy(c, d).wait_recv()
+        (codes,), unit = fixed([near_sum(c, 1 - y)])
+        tail_out[rds(c), :] = codes
+        tail_unit_out[c] = jnp.broadcast_to(unit, tail_unit_out.shape[1:])
+        tail_unit_copy(c).start()
+        tail_copy(c).start()
+        tile[mine, rds(c), :] = near_sum(c, y)
+
+    def stage_amp(c):
+        tail_unit_copy(c).wait_recv()
+        tail_copy(c).wait_recv()
         r = rds(c)
-        tile[theirs, r, :] += near[0, 1 - y, r, :] + near[1, 1 - y, r, :]
-        tail_copy(c).start()
-        tile[mine, r, :] += near[0, y, r, :] + near[1, y, r, :]
-
-    def stage_tail(c):
-        tail_copy(c).wait_recv()
-        tail_pass(c).start()
-
-    def stage_amp(c):
-        tail_pass(c).wait_recv()
-        r = rds(c)
-        total = tile[mine, r, :] + tail[r, :]
+        total = tile[mine, r, :] + tail[r, :].astype(jnp.float32) * tail_unit[c][0:1, 0:1]
         denominator = eps_rows[r, 0:1] + eps_cols
         amp[mine, r, :] = (total / denominator).astype(jnp.bfloat16)
         amp_y_copy(c).start()
 
-    def stage_amp_pass(c):
-        amp_y_copy(c).wait_recv()
-        amp_y_pass(c, x * NY + from_y).start()
-
     def stage_spread(c):
-        amp_y_pass(c, theirs).wait_recv()
+        amp_y_copy(c, theirs).wait_recv()
         for d in range(2):
             amp_x_copy(c, d).start()
 
@@ -273,10 +282,8 @@
                 for b in range(BLOCKS):
                     acc_copy(b).start()
 
-    stages = (
-        stage_tile, stage_gamma, stage_forward, stage_spread, stage_amp_pass, stage_amp, stage_tail, stage_sum, stage_near,
-    )
-    offsets = (0, 16, 14, 12, 10, 8, 6, 4, 2)
+    stages = (stage_tile, stage_gamma, stage_forward, stage_spread, stage_amp, stage_sum, stage_near)
+    offsets = (0, 14, 11, 8, 6, 4, 2)
 
     def tick(t, carry):
         for stage, offset in zip(stages, offsets):
@@ -334,12 +341,12 @@
         for d in range(2):
             far_copy(c, d).wait_send()
             near_copy(c, d).wait_send()
+            near_unit_copy(c, d).wait_send()
             amp_x_copy(c, d).wait_send()
             amp_f_copy(c, d, (x_prev, x_next)[d]).wait_send()
         tail_copy(c).wait_send()
-        tail_pass(c).wait_send()
+        tail_unit_copy(c).wait_send()
         amp_y_copy(c).wait_send()
-        amp_y_pass(c, x * NY + from_y).wait_send()
         return carry
 
     lax.fori_loop(0, n, sent, 0)
@@ -364,10 +371,14 @@
             pltpu.VMEM((BLOCKS, half_v, width), f32),
             pltpu.VMEM((NY, half_v, width), bf16),
             pltpu.VMEM((NY, half_v, width), bf16),
-            pltpu.VMEM((2, NY, half_v, width), f32),
-            pltpu.VMEM((half_v, width), f32),
-            pltpu.VMEM((half_v, width), f32),
-            pltpu.VMEM((half_v, width), bf16),
+            pltpu.VMEM((2, NY, half_v, width), jnp.int16),
+            pltpu.VMEM((2, NY, half_v, width), jnp.int16),
+            pltpu.VMEM((n, 2, 8, 128), f32),
+            pltpu.VMEM((n, 2, 8, 128), f32),
+            pltpu.VMEM((half_v, width), jnp.int16),
+            pltpu.VMEM((half_v, width), jnp.int16),
+            pltpu.VMEM((n, 8, 128), f32),
+            pltpu.VMEM((n, 8, 128), f32),
             pltpu.VMEM((BLOCKS, half_v, width), bf16),
             pltpu.VMEM((BLOCKS, width, NC * k), f32),
             pltpu.VMEM((half_v, NC * k), bf16),
@@ -381,7 +392,7 @@
             dma((half_v // PART, 2, 2)),
             dma((n, 2, 2)),
             dma((n, 2, 2)),
-            dma((n, 2)),
+            dma((n, 2, 2)),
             dma((n, 2)),
             dma((n, 2)),
             dma((n, 2)),

time: 144 us -> 131 us (0.910)
  Pallas kernels: 139 us -> 126 us
    pallas_call x1, Pallas kernels: 139 us -> 126 us  [per_device(): pl.pallas_call(functools.partial(kernel, n_occ, rows), out_shape=jax.Shap...]
where the time goes in v2:
time: 131 us; the launch traced here: 130 us
  Pallas kernels  126 us (96%)
  local copies, waits for them, and re-layouts  3.76 us (3%)
    pallas_call x1, Pallas kernels, per_device(): pl.pallas_call(functools.partial(kernel, n_occ, rows), out_shape=jax.Shap...  126 us
    unnamed x1, local copies, waits for them, and re-layouts  3.76 us

profile of v2, /device:TPU:1, one launch (start us, length us, event | category | flops | bytes accessed | tf_op | source)
XLA Modules:
  0.0 130.0 jit_solution(1556886886936820794)
XLA Ops:
  0.7 125.5 %shard_map.55 = f32[2048,384]{1,0:T(8,128)} custom-call(f32[32]{0:T(128)} %eps_occ.1, s32[1]{0:T(128)S(6)} %copy.7.start, s32[16]{0:T(128)} %assignment.1, bf16[2048,384]{1,0:T(8,128)(2,1)} %bitcast.4, f32[1,2048]{1,0:T(1,128)} %bitcast.5), custom_call_target="tpu_custom_call" | custom-call | flops 9663676416 | bytes 4718592 | tf_op jit(solution)/shard_map/pallas_call | solution.py:363
  126.2 3.8 %copy.8 = f32[1,2048,384]{2,1,0:T(8,128)} copy(f32[1,2048,384]{2,1,0:T(8,128)} %bitcast.3) | data formatting | bytes 6291456

commit v3 on v2

--- a/solution.py
+++ b/solution.py
@@ -33,7 +33,7 @@
     tail_out, tail, tail_unit_out, tail_unit, amp, acc, back, back_in, acc_in, eps_rows, right_last, amp_last,
     local_sem, left_sem, right_sem, far_sem, near_sem, near_unit_sem,
     tail_sem, tail_unit_sem,
-    amp_y_sem, amp_x_sem, amp_f_sem, back_sem, acc_sem, right_last_sem, amp_last_sem,
+    amp_x_sem, amp_f_sem, back_sem, acc_sem, right_last_sem, amp_last_sem,
 ):
     v, k = own.shape
     half_v = v // NC
@@ -57,7 +57,6 @@
     x_dev = (at(o, x_next, y, core), at(o, x_prev, y, core))
     next_dev = (at(o_next, x, y, 0), at(o_next, x, y, 1))
     prev_dev = (at(o_prev, x, y, 0), at(o_prev, x, y, 1))
-    mine, theirs = x * NY + y, x * NY + 1 - y
 
     def remote(src, dst, sem, device, there=None):
         return pltpu.make_async_remote_copy(
@@ -103,14 +102,10 @@
         return remote(near_unit_out.at[c, d], near_unit.at[c, d], near_unit_sem.at[c, d], x_dev[d])
 
     def tail_copy(c):
-        return remote(tail_out.at[rds(c), :], tail.at[rds(c), :], tail_sem.at[c], partner)
+        return remote(tail_out.at[:, rds(c), :], tail.at[:, rds(c), :], tail_sem.at[c], partner)
 
     def tail_unit_copy(c):
         return remote(tail_unit_out.at[c], tail_unit.at[c], tail_unit_sem.at[c], partner)
-
-    def amp_y_copy(c, block=mine):
-        block = amp.at[block, rds(c), :]
-        return remote(block, block, amp_y_sem.at[c], partner)
 
     def amp_x_copy(c, d, x_=x):
         block = amp.at[pair_of(x_), rds(c), :]
@@ -150,7 +145,9 @@
         acc[b] = jnp.zeros((width, NC * k), jnp.float32)
     slot = start[0]
     occ_sum = eps_occ[slot + assignment[o]] + eps_occ[slot + assignment[o_prev]]
-    eps_cols = eps_vir[:, pl.ds(pl.multiple_of(mine * width, width), width)] - occ_sum
+    eps_cols = [
+        eps_vir[:, pl.ds(pl.multiple_of((x * NY + j) * width, width), width)] - occ_sum for j in range(NY)
+    ]
 
     pl.semaphore_wait(barrier, len(others))
 
@@ -223,24 +220,24 @@
         for d in range(2):
             near_unit_copy(c, d).wait_recv()
             near_copy(c, d).wait_recv()
-        (codes,), unit = fixed([near_sum(c, 1 - y)])
-        tail_out[rds(c), :] = codes
+        sums = [near_sum(c, j) for j in range(NY)]
+        codes, unit = fixed(sums)
+        for j in range(NY):
+            tail_out[j, rds(c), :] = codes[j]
         tail_unit_out[c] = jnp.broadcast_to(unit, tail_unit_out.shape[1:])
         tail_unit_copy(c).start()
         tail_copy(c).start()
-        tile[mine, rds(c), :] = near_sum(c, y)
+        for j in range(NY):
+            tile[x * NY + j, rds(c), :] = sums[j]
 
     def stage_amp(c):
         tail_unit_copy(c).wait_recv()
         tail_copy(c).wait_recv()
         r = rds(c)
-        total = tile[mine, r, :] + tail[r, :].astype(jnp.float32) * tail_unit[c][0:1, 0:1]
-        denominator = eps_rows[r, 0:1] + eps_cols
-        amp[mine, r, :] = (total / denominator).astype(jnp.bfloat16)
-        amp_y_copy(c).start()
-
-    def stage_spread(c):
-        amp_y_copy(c, theirs).wait_recv()
+        for j in range(NY):
+            total = tile[x * NY + j, r, :] + tail[j, r, :].astype(jnp.float32) * tail_unit[c][0:1, 0:1]
+            denominator = eps_rows[r, 0:1] + eps_cols[j]
+            amp[x * NY + j, r, :] = (total / denominator).astype(jnp.bfloat16)
         for d in range(2):
             amp_x_copy(c, d).start()
 
@@ -282,8 +279,8 @@
                 for b in range(BLOCKS):
                     acc_copy(b).start()
 
-    stages = (stage_tile, stage_gamma, stage_forward, stage_spread, stage_amp, stage_sum, stage_near)
-    offsets = (0, 14, 11, 8, 6, 4, 2)
+    stages = (stage_tile, stage_gamma, stage_forward, stage_amp, stage_sum, stage_near)
+    offsets = (0, 11, 9, 6, 3, 1)
 
     def tick(t, carry):
         for stage, offset in zip(stages, offsets):
@@ -346,7 +343,6 @@
             amp_f_copy(c, d, (x_prev, x_next)[d]).wait_send()
         tail_copy(c).wait_send()
         tail_unit_copy(c).wait_send()
-        amp_y_copy(c).wait_send()
         return carry
 
     lax.fori_loop(0, n, sent, 0)
@@ -375,8 +371,8 @@
             pltpu.VMEM((2, NY, half_v, width), jnp.int16),
             pltpu.VMEM((n, 2, 8, 128), f32),
             pltpu.VMEM((n, 2, 8, 128), f32),
-            pltpu.VMEM((half_v, width), jnp.int16),
-            pltpu.VMEM((half_v, width), jnp.int16),
+            pltpu.VMEM((NY, half_v, width), jnp.int16),
+            pltpu.VMEM((NY, half_v, width), jnp.int16),
             pltpu.VMEM((n, 8, 128), f32),
             pltpu.VMEM((n, 8, 128), f32),
             pltpu.VMEM((BLOCKS, half_v, width), bf16),
@@ -395,7 +391,6 @@
             dma((n, 2, 2)),
             dma((n, 2)),
             dma((n, 2)),
-            dma((n, 2)),
             dma((n, 2, 2)),
             dma((n, 2, 2)),
             dma((half_v // PART, 2, 2)),

time: 131 us -> 135 us (1.031)
  Pallas kernels: 126 us -> 130 us
    pallas_call x1, Pallas kernels: 126 us -> 130 us  [per_device(): pl.pallas_call(functools.partial(kernel, n_occ, rows), out_shape=jax.Shap...]
where the time goes in v3:
time: 135 us; the launch traced here: 134 us
  Pallas kernels  130 us (96%)
  local copies, waits for them, and re-layouts  3.76 us (3%)
    pallas_call x1, Pallas kernels, per_device(): pl.pallas_call(functools.partial(kernel, n_occ, rows), out_shape=jax.Shap...  130 us
    unnamed x1, local copies, waits for them, and re-layouts  3.76 us

profile of v3, /device:TPU:1, one launch (start us, length us, event | category | flops | bytes accessed | tf_op | source)
XLA Modules:
  0.0 134.3 jit_solution(8612406937836289501)
XLA Ops:
  0.7 129.9 %shard_map.55 = f32[2048,384]{1,0:T(8,128)} custom-call(f32[32]{0:T(128)} %eps_occ.1, s32[1]{0:T(128)S(6)} %copy.7.start, s32[16]{0:T(128)} %assignment.1, bf16[2048,384]{1,0:T(8,128)(2,1)} %bitcast.4, f32[1,2048]{1,0:T(1,128)} %bitcast.5), custom_call_target="tpu_custom_call" | custom-call | flops 9663676416 | bytes 4718592 | tf_op jit(solution)/shard_map/pallas_call | solution.py:359
  130.6 3.8 %copy.8 = f32[1,2048,384]{2,1,0:T(8,128)} copy(f32[1,2048,384]{2,1,0:T(8,128)} %bitcast.3) | data formatting | bytes 6291456

commit v4 on v3

--- a/solution.py
+++ b/solution.py
@@ -280,7 +280,7 @@
                     acc_copy(b).start()
 
     stages = (stage_tile, stage_gamma, stage_forward, stage_amp, stage_sum, stage_near)
-    offsets = (0, 11, 9, 6, 3, 1)
+    offsets = (0, 14, 11, 8, 5, 2)
 
     def tick(t, carry):
         for stage, offset in zip(stages, offsets):

time: 135 us -> 132 us (0.978)
  Pallas kernels: 130 us -> 127 us
    pallas_call x1, Pallas kernels: 130 us -> 127 us  [per_device(): pl.pallas_call(functools.partial(kernel, n_occ, rows), out_shape=jax.Shap...]
where the time goes in v4:
time: 132 us
  Pallas kernels  127 us (96%)
  local copies, waits for them, and re-layouts  3.76 us (3%)
    pallas_call x1, Pallas kernels, per_device(): pl.pallas_call(functools.partial(kernel, n_occ, rows), out_shape=jax.Shap...  127 us
    unnamed x1, local copies, waits for them, and re-layouts  3.76 us

profile of v4, /device:TPU:1, one launch (start us, length us, event | category | flops | bytes accessed | tf_op | source)
XLA Modules:
  0.0 131.6 jit_solution(18119559257579523983)
XLA Ops:
  0.7 127.2 %shard_map.55 = f32[2048,384]{1,0:T(8,128)} custom-call(f32[32]{0:T(128)} %eps_occ.1, s32[1]{0:T(128)S(6)} %copy.7.start, s32[16]{0:T(128)} %assignment.1, bf16[2048,384]{1,0:T(8,128)(2,1)} %bitcast.4, f32[1,2048]{1,0:T(1,128)} %bitcast.5), custom_call_target="tpu_custom_call" | custom-call | flops 9663676416 | bytes 4718592 | tf_op jit(solution)/shard_map/pallas_call | solution.py:359
  127.8 3.8 %copy.8 = f32[1,2048,384]{2,1,0:T(8,128)} copy(f32[1,2048,384]{2,1,0:T(8,128)} %bitcast.3) | data formatting | bytes 6291456

commit v5 on v4

--- a/solution.py
+++ b/solution.py
@@ -10,6 +10,7 @@
 MESH = pl.DeviceIdType.MESH
 NX, NY, NC = 4, 2, 2
 BLOCKS = NX * NY
+Y_LO, Y_ALL = 2, 4
 ROWS = 64
 PART = 64
 GROUP = 256
@@ -30,9 +31,9 @@
 def kernel(
     n_occ, rows, eps_occ, start, assignment, own, eps_vir, out,
     left, right, tile, far_out, far, near_out, near, near_unit_out, near_unit,
-    tail_out, tail, tail_unit_out, tail_unit, amp, acc, back, back_in, acc_in, eps_rows, right_last, amp_last,
+    tail_out, tail, tail_unit_out, tail_unit, tail_via, tail_unit_via, amp, acc, back, back_in, acc_in, eps_rows, right_last, amp_last,
     local_sem, left_sem, right_sem, far_sem, near_sem, near_unit_sem,
-    tail_sem, tail_unit_sem,
+    tail_sem, tail_unit_sem, tail_via_sem, tail_unit_via_sem,
     amp_x_sem, amp_f_sem, back_sem, acc_sem, right_last_sem, amp_last_sem,
 ):
     v, k = own.shape
@@ -53,7 +54,11 @@
         return (o_, (x_ * NY + y_) * NC + c_)
 
     sibling = at(o, x, y, 1 - core)
-    partner = at(o, x, 1 - y, core)
+    def across(step):
+        place = lax.rem(y * Y_LO + lax.rem(o, Y_LO) + step + Y_ALL, Y_ALL)
+        return at((o // Y_LO) * Y_LO + lax.rem(place, Y_LO), x, place // Y_LO, core)
+
+    hop, hop_back = across(1 - 2 * core), across(2 * core - 1)
     x_dev = (at(o, x_next, y, core), at(o, x_prev, y, core))
     next_dev = (at(o_next, x, y, 0), at(o_next, x, y, 1))
     prev_dev = (at(o_prev, x, y, 0), at(o_prev, x, y, 1))
@@ -102,10 +107,16 @@
         return remote(near_unit_out.at[c, d], near_unit.at[c, d], near_unit_sem.at[c, d], x_dev[d])
 
     def tail_copy(c):
-        return remote(tail_out.at[:, rds(c), :], tail.at[:, rds(c), :], tail_sem.at[c], partner)
+        return remote(tail_out.at[:, rds(c), :], tail_via.at[:, rds(c), :], tail_via_sem.at[c], hop)
 
     def tail_unit_copy(c):
-        return remote(tail_unit_out.at[c], tail_unit.at[c], tail_unit_sem.at[c], partner)
+        return remote(tail_unit_out.at[c], tail_unit_via.at[c], tail_unit_via_sem.at[c], hop)
+
+    def tail_pass(c):
+        return remote(tail_via.at[:, rds(c), :], tail.at[:, rds(c), :], tail_sem.at[c], hop)
+
+    def tail_unit_pass(c):
+        return remote(tail_unit_via.at[c], tail_unit.at[c], tail_unit_sem.at[c], hop)
 
     def amp_x_copy(c, d, x_=x):
         block = amp.at[pair_of(x_), rds(c), :]
@@ -131,7 +142,7 @@
         return remote(acc.at[b, :, cols(1 - core)], acc_in.at[b], acc_sem.at[b], sibling)
 
     barrier = pltpu.get_barrier_semaphore()
-    others = (sibling, partner) + x_dev + next_dev + prev_dev
+    others = (sibling, hop, hop_back) + x_dev + next_dev + prev_dev
     for device in others:
         pl.semaphore_signal(barrier, inc=1, device_id=device, device_id_type=MESH)
     local = pltpu.make_async_copy(own, left.at[:, cols(core)], local_sem)
@@ -230,9 +241,15 @@
         for j in range(NY):
             tile[x * NY + j, rds(c), :] = sums[j]
 
+    def stage_tail(c):
+        tail_unit_copy(c).wait_recv()
+        tail_unit_pass(c).start()
+        tail_copy(c).wait_recv()
+        tail_pass(c).start()
+
     def stage_amp(c):
-        tail_unit_copy(c).wait_recv()
-        tail_copy(c).wait_recv()
+        tail_unit_pass(c).wait_recv()
+        tail_pass(c).wait_recv()
         r = rds(c)
         for j in range(NY):
             total = tile[x * NY + j, r, :] + tail[j, r, :].astype(jnp.float32) * tail_unit[c][0:1, 0:1]
@@ -279,8 +296,8 @@
                 for b in range(BLOCKS):
                     acc_copy(b).start()
 
-    stages = (stage_tile, stage_gamma, stage_forward, stage_amp, stage_sum, stage_near)
-    offsets = (0, 14, 11, 8, 5, 2)
+    stages = (stage_tile, stage_gamma, stage_forward, stage_amp, stage_tail, stage_sum, stage_near)
+    offsets = (0, 15, 12, 9, 6, 4, 2)
 
     def tick(t, carry):
         for stage, offset in zip(stages, offsets):
@@ -343,6 +360,8 @@
             amp_f_copy(c, d, (x_prev, x_next)[d]).wait_send()
         tail_copy(c).wait_send()
         tail_unit_copy(c).wait_send()
+        tail_pass(c).wait_send()
+        tail_unit_pass(c).wait_send()
         return carry
 
     lax.fori_loop(0, n, sent, 0)
@@ -375,6 +394,8 @@
             pltpu.VMEM((NY, half_v, width), jnp.int16),
             pltpu.VMEM((n, 8, 128), f32),
             pltpu.VMEM((n, 8, 128), f32),
+            pltpu.VMEM((NY, half_v, width), jnp.int16),
+            pltpu.VMEM((n, 8, 128), f32),
             pltpu.VMEM((BLOCKS, half_v, width), bf16),
             pltpu.VMEM((BLOCKS, width, NC * k), f32),
             pltpu.VMEM((half_v, NC * k), bf16),
@@ -389,6 +410,8 @@
             dma((n, 2, 2)),
             dma((n, 2, 2)),
             dma((n, 2, 2)),
+            dma((n, 2)),
+            dma((n, 2)),
             dma((n, 2)),
             dma((n, 2)),
             dma((n, 2, 2)),

time: 132 us -> 132 us (level)
  no operation moved by 1% of the time
where the time goes in v5:
time: 132 us
  Pallas kernels  128 us (97%)
  local copies, waits for them, and re-layouts  3.76 us (3%)
    pallas_call x1, Pallas kernels, per_device(): pl.pallas_call(functools.partial(kernel, n_occ, rows), out_shape=jax.Shap...  128 us
    unnamed x1, local copies, waits for them, and re-layouts  3.76 us

profile of v5, /device:TPU:1, one launch (start us, length us, event | category | flops | bytes accessed | tf_op | source)
XLA Modules:
  0.0 132.0 jit_solution(12893039131683010206)
XLA Ops:
  0.7 127.6 %shard_map.55 = f32[2048,384]{1,0:T(8,128)} custom-call(f32[32]{0:T(128)} %eps_occ.1, s32[1]{0:T(128)S(6)} %copy.7.start, s32[16]{0:T(128)} %assignment.1, bf16[2048,384]{1,0:T(8,128)(2,1)} %bitcast.4, f32[1,2048]{1,0:T(1,128)} %bitcast.5), custom_call_target="tpu_custom_call" | custom-call | flops 9663676416 | bytes 4718592 | tf_op jit(solution)/shard_map/pallas_call | solution.py:378
  128.3 3.8 %copy.8 = f32[1,2048,384]{2,1,0:T(8,128)} copy(f32[1,2048,384]{2,1,0:T(8,128)} %bitcast.3) | data formatting | bytes 6291456

commit v6 on v2

--- a/solution.py
+++ b/solution.py
@@ -11,9 +11,9 @@
 NX, NY, NC = 4, 2, 2
 BLOCKS = NX * NY
 ROWS = 64
-PART = 64
+PART = 128
 GROUP = 256
-AHEAD = 4
+AHEAD = 2
 
 
 def dot(a, b, dims):

time: 131 us -> 137 us (1.046)
  Pallas kernels: 126 us -> 131 us
    pallas_call x1, Pallas kernels: 126 us -> 131 us  [per_device(): pl.pallas_call(functools.partial(kernel, n_occ, rows), out_shape=jax.Shap...]
where the time goes in v6:
time: 137 us; the launch traced here: 135 us
  Pallas kernels  131 us (96%)
  local copies, waits for them, and re-layouts  3.76 us (3%)
    pallas_call x1, Pallas kernels, per_device(): pl.pallas_call(functools.partial(kernel, n_occ, rows), out_shape=jax.Shap...  131 us
    unnamed x1, local copies, waits for them, and re-layouts  3.76 us

profile of v6, /device:TPU:1, one launch (start us, length us, event | category | flops | bytes accessed | tf_op | source)
XLA Modules:
  0.0 135.4 jit_solution(9250520612007942514)
XLA Ops:
  0.7 131.0 %shard_map.55 = f32[2048,384]{1,0:T(8,128)} custom-call(f32[32]{0:T(128)} %eps_occ.1, s32[1]{0:T(128)S(6)} %copy.7.start, s32[16]{0:T(128)} %assignment.1, bf16[2048,384]{1,0:T(8,128)(2,1)} %bitcast.4, f32[1,2048]{1,0:T(1,128)} %bitcast.5), custom_call_target="tpu_custom_call" | custom-call | flops 9663676416 | bytes 4718592 | tf_op jit(solution)/shard_map/pallas_call | solution.py:363
  131.7 3.8 %copy.8 = f32[1,2048,384]{2,1,0:T(8,128)} copy(f32[1,2048,384]{2,1,0:T(8,128)} %bitcast.3) | data formatting | bytes 6291456
